TPU v7x, 512 devices: a whole 4x4x16 slice. The times are simulated.
512 devices in a mesh: harm: 8 (over x, z_hi), row: 64 (over z_lo, y, core).
Axes of the slice: x: 4, y: 4, z: 16 (z_hi: 2, z_lo: 8; z = z_hi * 8 + z_lo), core: 2. Of those that a mesh axis runs over, the one named last changes fastest.
Arguments:
- currents: float32 [8, 4, 2, 512, 512], P('harm', None, None, 'row'), may hold values from -6 to 6
- incident: float32 [8, 4, 2, 512, 512], P('harm', None, None, 'row'), may hold values from -6 to 6
- kernel: float32 [8, 4, 4, 2, 1024, 1024], P('harm', None, None, None, 'row'), may hold values from -4 to 4
- port_weights: float32 [4], replicated, may hold values from 0.2 to 0.6
- bias_level: int32 [512, 512], P('row', 'harm'), may hold values from 0 to 15
Outputs:
- residual: float32 [8, 4, 2, 512, 512], P('harm', None, None, 'row')
Inputs may be any that keep to these rules, and one draw needn't show every extreme that they name: `bias_level`: integer capacitance level of each cell's varactor.
All inputs are finite; a program needn't handle non-finite values.
Results may differ from a plain program's by a relative error of at most 0.0003.
Values sent between devices are 32-bit elements; how exact they have to be, the bound alone decides.
A program may use at most 64 MiB of HBM per device.

v0:
```python
import functools
import math

import jax
import jax.numpy as jnp
import ml_dtypes
import numpy as np
from jax import lax
from jax.experimental import pallas as pl
from jax.experimental.pallas import tpu as pltpu
from jax.sharding import PartitionSpec as P

MESH = pl.DeviceIdType.MESH
F32 = jnp.float32
BF16 = jnp.bfloat16
HARMS = 8
SAMPLES = 32
NROW = 64
PAD = 1024


def split_np(table):
    high = table.astype(ml_dtypes.bfloat16)
    low = (table - high.astype(np.float64)).astype(ml_dtypes.bfloat16)
    return high, low


def cos_sin(product, length):
    angle = 2.0 * np.pi / length * (product % length).astype(np.float64)
    return np.cos(angle), np.sin(angle)


@functools.lru_cache(maxsize=None)
def tables():
    c, s = cos_sin(np.arange(512)[:, None] * np.arange(PAD)[None, :], PAD)
    w = np.concatenate([c.reshape(512, 4, 256), s.reshape(512, 4, 256)], axis=2).transpose(1, 0, 2)
    w1 = np.stack(split_np(w))
    r = 8 * np.arange(64)[None, :, None] + np.arange(8)[:, None, None]
    c, s = cos_sin(r * np.arange(128)[None, None, :], PAD)
    hi, lo = split_np(np.concatenate([c, s], axis=2))
    e2 = np.concatenate([hi, hi, lo], axis=1)
    c, s = cos_sin(r * np.arange(128)[None, None, :], PAD)
    hi, lo = split_np(np.concatenate([c, s], axis=1) / float(PAD * PAD))
    e3 = np.concatenate([hi, hi, lo], axis=2)
    c, s = cos_sin(np.arange(PAD)[:, None] * np.arange(512)[None, :], PAD)
    w = np.concatenate([c.reshape(PAD, 4, 128), s.reshape(PAD, 4, 128)], axis=2).transpose(1, 0, 2)
    w4 = np.stack(split_np(w))
    k = np.stack([2 * np.arange(4) + 2, 2 * np.arange(4) + 1], axis=1)
    c, s = cos_sin(k[:, None, :] * np.arange(16)[None, :, None], SAMPLES)
    co = np.stack([c, s]) * (2.0 / SAMPLES)
    coef = np.repeat(co, 64, axis=3).astype(np.float32).reshape(128, 128)
    return w1, e2, e3, w4, coef


def dft8(z, sign):
    def add(a, b):
        return (a[0] + b[0], a[1] + b[1])

    def sub(a, b):
        return (a[0] - b[0], a[1] - b[1])

    def turn(a):
        return (-a[1], a[0]) if sign > 0 else (a[1], -a[0])

    def four(a0, a1, a2, a3):
        p, m = add(a0, a2), sub(a0, a2)
        q, d = add(a1, a3), turn(sub(a1, a3))
        return [add(p, q), add(m, d), sub(p, q), sub(m, d)]

    even = four(z[0], z[2], z[4], z[6])
    odd = four(z[1], z[3], z[5], z[7])
    h = math.sqrt(0.5)
    o1, o3 = turn(odd[1]), turn(odd[3])
    odd = [
        odd[0],
        ((odd[1][0] + o1[0]) * h, (odd[1][1] + o1[1]) * h),
        turn(odd[2]),
        ((o3[0] - odd[3][0]) * h, (o3[1] - odd[3][1]) * h),
    ]
    return [add(e, o) for e, o in zip(even, odd)] + [sub(e, o) for e, o in zip(even, odd)]


def split(x):
    high = x.astype(BF16)
    return high, (x - high.astype(F32)).astype(BF16)


def lanes_of(shape):
    return lax.broadcasted_iota(jnp.int32, shape, 1)


def swap_blocks(v):
    v = list(v)
    block = lanes_of(v[0].shape) // 16
    for s in (4, 2, 1):
        keep = (block & s) == 0
        for a in range(8):
            if a & s:
                continue
            x, y = v[a], v[a + s]
            v[a] = jnp.where(keep, x, pltpu.roll(y, 16 * s, 1))
            v[a + s] = jnp.where(keep, pltpu.roll(x, 128 - 16 * s, 1), y)
    return v


def halves(x, y):
    left = lanes_of(x.shape) < 64
    return (
        jnp.where(left, x, pltpu.roll(y, 64, 1)),
        jnp.where(left, pltpu.roll(x, 64, 1), y),
    )


def dot(a, b, ca=1, cb=0):
    return lax.dot_general(a, b, (((ca,), (cb,)), ((), ())), preferred_element_type=F32)


def tile(ref, i):
    return ref.at[pl.ds(pl.multiple_of(8 * i, 8), 8), :]


def spread(axis, count, src, dst, send, recv):
    me = lax.axis_index(axis)

    def step(i, carry):
        to = lax.rem(me + i, count)
        pltpu.make_async_remote_copy(
            src_ref=tile(src, to),
            dst_ref=tile(dst, me),
            send_sem=send,
            recv_sem=recv,
            device_id={axis: to},
            device_id_type=MESH,
        ).start()
        return carry

    lax.fori_loop(1, count, step, 0)
    tile(dst, me)[...] = tile(src, me)[...]


def settle(count, src, dst, send, recv):
    rows = pl.ds(0, 8 * (count - 1))
    pltpu.make_async_copy(dst.at[rows], dst.at[rows], recv).wait()
    pltpu.make_async_copy(src.at[rows], src.at[rows], send).wait()


def kernel(
    cur, inc, bias, coef, pw, g_hbm, w1_hbm, e2_hbm, e3_hbm, w4_hbm, out,
    g, w1, e2, e3, w4, tx1, rx1, zb, yb, tx2, rx2, xk, tot, hs, hr, ds, dr, load, send, recv,
):
    row, harm = lax.axis_index("row"), lax.axis_index("harm")
    loads = [
        pltpu.make_async_copy(a, b, load.at[i])
        for i, (a, b) in enumerate(((w1_hbm, w1), (e2_hbm, e2), (g_hbm, g), (e3_hbm, e3), (w4_hbm, w4)))
    ]
    for c in loads:
        c.start()
    barrier = pltpu.get_barrier_semaphore()

    def greet(axis, me, count):
        def step(i, carry):
            pl.semaphore_signal(
                barrier, inc=1, device_id={axis: lax.rem(me + i, count)}, device_id_type=MESH
            )
            return carry

        lax.fori_loop(1, count, step, 0)

    greet("harm", harm, HARMS)
    greet("row", row, NROW)

    loads[0].wait()
    hi, lo = split(cur[...].reshape(64, 512))
    both = jnp.concatenate([hi, lo], axis=0)
    for j in range(4):
        r1 = dot(both, w1[0, j])
        r = r1[:64] + r1[64:] + dot(hi, w1[1, j])
        r = r.reshape(4, 2, 8, 512)
        for half in range(2):
            c, s = r[..., 128 * half : 128 * half + 128], r[..., 256 + 128 * half : 384 + 128 * half]
            v = [c[b, 0] + s[b, 1] for b in range(4)] + [c[b, 1] - s[b, 0] for b in range(4)]
            for i, x in enumerate(swap_blocks(v)):
                d = 16 * j + 8 * half + i
                tx1[8 * d : 8 * d + 8, :] = x

    pl.semaphore_wait(barrier, HARMS + NROW - 2)
    spread("row", NROW, tx1, rx1, send.at[0], recv.at[0])
    loads[1].wait()
    loads[2].wait()
    settle(NROW, tx1, rx1, send.at[0], recv.at[0])

    def rows_forward(t, carry):
        hi, lo = split(rx1[pl.ds(t, 64, stride=8), :])
        r = dot(jnp.concatenate([hi, lo, hi], axis=0), e2[t], 0, 0)
        p, q = r[:, :128], r[:, 128:]
        zb[t, 0] = p[:64] + q[64:]
        zb[t, 1] = p[64:] - q[:64]
        return carry

    lax.fori_loop(0, 8, rows_forward, 0)

    def combine(i, carry):
        at = pl.ds(pl.multiple_of(8 * i, 8), 8)
        z = dft8([(zb[t, 0, at, :], zb[t, 1, at, :]) for t in range(8)], -1)
        for q in range(8):
            zb[q, 0, at, :], zb[q, 1, at, :] = z[q]
        return carry

    lax.fori_loop(0, 8, combine, 0)

    def mix(i, carry):
        b, kh = i // 2, i % 2
        at = pl.ds(pl.multiple_of(8 * kh, 8), 8)
        f = []
        for q in range(8):
            re = im = None
            for c in range(4):
                src = pl.ds(pl.multiple_of(16 * c + 8 * kh, 8), 8)
                sr, si = zb[q, 0, src, :], zb[q, 1, src, :]
                gr = g[b, c, 0, at, 128 * q : 128 * q + 128]
                gi = g[b, c, 1, at, 128 * q : 128 * q + 128]
                x, y = gr * sr - gi * si, gr * si + gi * sr
                re, im = (x, y) if c == 0 else (re + x, im + y)
            f.append((re, im))
        y = dft8(f, 1)
        for t in range(8):
            yb[t, pl.ds(pl.multiple_of(8 * i, 8), 8), :] = y[t][0]
            yb[t, pl.ds(pl.multiple_of(64 + 8 * i, 8), 8), :] = y[t][1]
        return carry

    lax.fori_loop(0, 8, mix, 0)
    loads[3].wait()

    def rows_inverse(t, carry):
        hi, lo = split(yb[t])
        r = dot(e3[t], jnp.concatenate([hi, lo, hi], axis=1), 1, 1)
        turned = pltpu.roll(r[64:], 64, 1)
        left = lanes_of(turned.shape) < 64
        tx2[pl.ds(t, 64, stride=8), :] = r[:64] + jnp.where(left, -turned, turned)
        return carry

    lax.fori_loop(0, 8, rows_inverse, 0)
    spread("row", NROW, tx2, rx2, send.at[1], recv.at[1])
    loads[4].wait()
    settle(NROW, tx2, rx2, send.at[1], recv.at[1])

    for j in range(8):
        v = swap_blocks([rx2[64 * j + 8 * i : 64 * j + 8 * i + 8, :] for i in range(8)])
        for i in range(8):
            xk[8 * i : 8 * i + 8, 128 * j : 128 * j + 128] = v[i]
    hi, lo = split(xk[...])
    both = jnp.concatenate([hi, lo], axis=0)
    for u in range(4):
        r1 = dot(both, w4[0, u])
        r = r1[:64] + r1[64:] + dot(hi, w4[1, u])
        fields = (r[:32, :128] - r[32:, 128:], r[32:, :128] + r[:32, 128:])
        at = slice(128 * u, 128 * u + 128)
        volt = []
        for p in range(2):
            acc = None
            for b in range(4):
                x = fields[p][8 * b : 8 * b + 8] + inc[b, p, :, at]
                tot[b, p, :, at] = x
                acc = pw[b] * x if b == 0 else acc + pw[b] * x
            volt.append(acc)
        hs[16 * u : 16 * u + 8, :], hs[16 * u + 8 : 16 * u + 16, :] = halves(*volt)

    spread("harm", HARMS, hs, hr, send.at[2], recv.at[2])
    settle(HARMS, hs, hr, send.at[2], recv.at[2])

    left = lanes_of((8, 128)) < 64
    sign = jnp.where(left, 1.0, -1.0)
    volts = []
    for h in range(HARMS):
        v = hr[8 * h : 8 * h + 8, :]
        w = pltpu.roll(v, 64, 1)
        v0, v1 = jnp.where(left, v, w), jnp.where(left, w, v)
        if h % 2 == 0:
            v0, v1 = v0 * sign, v1 * sign
        volts.append((v0, v1))
    level = bias[...].astype(F32)
    cap = 0.05 + 0.02 * jnp.concatenate([level, level], axis=1)
    sums = [[None] * 4 for _ in range(4)]
    for n in range(16):
        wave = None
        for h in range(HARMS):
            angle = 2.0 * math.pi * (((h + 1) * n) % SAMPLES) / SAMPLES
            x = volts[h][0] * math.cos(angle) - volts[h][1] * math.sin(angle)
            wave = x if wave is None else wave + x
        conduct = 0.05 * (jnp.exp(wave * 0.25) - 1.0)
        charge = cap * (wave + 0.2 * wave * wave)
        conduct = conduct * sign + pltpu.roll(conduct, 64, 1)
        charge = charge * sign + pltpu.roll(charge, 64, 1)
        for j in range(4):
            cs = coef[16 * j + n : 16 * j + n + 1, :]
            sn = coef[64 + 16 * j + n : 64 + 16 * j + n + 1, :]
            terms = (conduct * cs, conduct * sn, charge * cs, charge * sn)
            sums[j] = [t if a is None else a + t for a, t in zip(sums[j], terms)]
    for j in range(4):
        order = jnp.where(left, 0.25 * (2 * j + 2), 0.25 * (2 * j + 1))
        cc, cn, qc, qn = sums[j]
        even, odd = halves(cc + order * qn, order * qc - cn)
        ds[16 * j : 16 * j + 8, :] = odd
        ds[16 * j + 8 : 16 * j + 16, :] = even

    spread("harm", HARMS, ds, dr, send.at[3], recv.at[3])
    settle(HARMS, ds, dr, send.at[3], recv.at[3])
    for u in range(4):
        diode = halves(dr[16 * u : 16 * u + 8, :], dr[16 * u + 8 : 16 * u + 16, :])
        at = slice(128 * u, 128 * u + 128)
        for b in range(4):
            for p in range(2):
                out[b, p, :, at] = tot[b, p, :, at] - pw[b] * diode[p]


def body(currents, incident, green, port_weights, bias_level):
    w1, e2, e3, w4, coef = (jnp.asarray(t) for t in tables())
    vmem = pl.BlockSpec(memory_space=pltpu.VMEM)
    smem = pl.BlockSpec(memory_space=pltpu.SMEM)
    anyw = pl.BlockSpec(memory_space=pl.ANY)
    out = pl.pallas_call(
        kernel,
        out_shape=jax.ShapeDtypeStruct((4, 2, 8, 512), F32),
        in_specs=[vmem, vmem, vmem, vmem, smem] + [anyw] * 5,
        out_specs=vmem,
        scratch_shapes=[
            pltpu.VMEM((4, 4, 2, 16, 1024), F32),
            pltpu.VMEM(w1.shape, BF16),
            pltpu.VMEM(e2.shape, BF16),
            pltpu.VMEM(e3.shape, BF16),
            pltpu.VMEM(w4.shape, BF16),
            pltpu.VMEM((512, 128), F32),
            pltpu.VMEM((512, 128), F32),
            pltpu.VMEM((8, 2, 64, 128), F32),
            pltpu.VMEM((8, 128, 128), F32),
            pltpu.VMEM((512, 128), F32),
            pltpu.VMEM((512, 128), F32),
            pltpu.VMEM((64, 1024), F32),
            pltpu.VMEM((4, 2, 8, 512), F32),
            pltpu.VMEM((64, 128), F32),
            pltpu.VMEM((64, 128), F32),
            pltpu.VMEM((64, 128), F32),
            pltpu.VMEM((64, 128), F32),
            pltpu.SemaphoreType.DMA((5,)),
            pltpu.SemaphoreType.DMA((4,)),
            pltpu.SemaphoreType.DMA((4,)),
        ],
        compiler_params=pltpu.CompilerParams(
            collective_id=0, has_side_effects=True, vmem_limit_bytes=48 * 2**20
        ),
        cost_estimate=pl.CostEstimate(flops=5 * 10**9, bytes_accessed=13 * 10**6, transcendentals=16384),
    )(currents[0], incident[0], bias_level, coef, port_weights, green[0], w1, e2, e3, w4)
    return out[None]


def solution(mesh):
    placed = (
        P("harm", None, None, "row", None),
        P("harm", None, None, "row", None),
        P("harm", None, None, None, "row", None),
        P(),
        P("row", "harm"),
    )
    return jax.shard_map(
        body,
        mesh=mesh,
        in_specs=placed,
        out_specs=P("harm", None, None, "row", None),
        check_vma=False,
    )
```

profile of v0, /device:TPU:96, one launch (start us, length us, event | category | flops | bytes accessed | tf_op | source)
XLA Modules:
  0.0 75.5 jit_solution(13643286504599322431)
XLA Ops:
  0.0 0.0 copy-start
  0.0 1.6 %copy-done = f32[1,4,4,2,16,1024]{5,4,3,2,1,0:T(8,128)S(1)} copy-done((f32[1,4,4,2,16,1024]{5,4,3,2,1,0:T(8,128)S(1)}, f32[1,4,4,2,16,1024]{5,4,3,2,1,0:T(8,128)}, u32[]{:S(2)}) %copy-start) | copy-done | bytes 2097176
  1.6 0.0 copy-start.1
  1.6 0.9 %copy-done.1 = f32[1,4,2,8,512]{4,3,2,1,0:T(8,128)S(1)} copy-done((f32[1,4,2,8,512]{4,3,2,1,0:T(8,128)S(1)}, f32[1,4,2,8,512]{4,3,2,1,0:T(8,128)}, u32[]{:S(2)}) %copy-start.1) | copy-done | bytes 131096
  2.5 0.0 copy-start.2
  2.5 0.9 %copy-done.2 = f32[1,4,2,8,512]{4,3,2,1,0:T(8,128)S(1)} copy-done((f32[1,4,2,8,512]{4,3,2,1,0:T(8,128)S(1)}, f32[1,4,2,8,512]{4,3,2,1,0:T(8,128)}, u32[]{:S(2)}) %copy-start.2) | copy-done | bytes 131096
  3.4 0.0 copy-start.3
  3.4 0.7 copy-done.3
  4.1 0.0 copy-start.4
  4.1 0.7 copy-done.4
  4.7 0.0 copy-start.5
  4.7 1.1 %copy-done.5 = bf16[8,128,384]{2,1,0:T(8,128)(2,1)S(1)} copy-done((bf16[8,128,384]{2,1,0:T(8,128)(2,1)S(1)}, bf16[8,128,384]{2,1,0:T(8,128)(2,1)}, u32[]{:S(2)}) %copy-start.5) | copy-done | bytes 786456
  5.9 0.0 copy-start.6
  5.9 1.1 %copy-done.6 = bf16[8,192,256]{2,1,0:T(8,128)(2,1)S(1)} copy-done((bf16[8,192,256]{2,1,0:T(8,128)(2,1)S(1)}, bf16[8,192,256]{2,1,0:T(8,128)(2,1)}, u32[]{:S(2)}) %copy-start.6) | copy-done | bytes 786456
  7.0 0.0 copy-start.7
  7.0 0.8 %copy-done.7 = f32[128,128]{1,0:T(8,128)S(1)} copy-done((f32[128,128]{1,0:T(8,128)S(1)}, f32[128,128]{1,0:T(8,128)}, u32[]{:S(2)}) %copy-start.7) | copy-done | bytes 65560
  7.9 67.0 %shard_map.100 = f32[4,2,8,512]{3,2,1,0:T(8,128)S(1)} custom-call(f32[4,2,8,512]{3,2,1,0:T(8,128)S(1)} %bitcast.6, f32[4,2,8,512]{3,2,1,0:T(8,128)S(1)} %bitcast.7, s32[8,64]{1,0:T(8,128)S(1)} %copy-done.3, f32[128,128]{1,0:T(8,128)S(1)} %copy-done.7, f32[4]{0:T(128)S(1)} %copy-done.4, f32[4,4,2,16,1024]{4,3,2,1,0:T(8,128)S(1)} %bitcast.5, ...), custom_call_target="tpu_custom_call" | custom-call | flops 5000000000 | bytes 13000000 | tf_op jit(solution)/shard_map/pallas_call | solution.py:321
  74.9 0.7 copy.12
Async XLA Ops:
  0.0 1.6 %copy-start = (f32[1,4,4,2,16,1024]{5,4,3,2,1,0:T(8,128)S(1)}, f32[1,4,4,2,16,1024]{5,4,3,2,1,0:T(8,128)}, u32[]{:S(2)}) copy-start(f32[1,4,4,2,16,1024]{5,4,3,2,1,0:T(8,128)} %param.12) | copy-start | bytes 6291460
  1.6 0.9 %copy-start.1 = (f32[1,4,2,8,512]{4,3,2,1,0:T(8,128)S(1)}, f32[1,4,2,8,512]{4,3,2,1,0:T(8,128)}, u32[]{:S(2)}) copy-start(f32[1,4,2,8,512]{4,3,2,1,0:T(8,128)} %param.10) | copy-start | bytes 393220
  2.5 0.9 %copy-start.2 = (f32[1,4,2,8,512]{4,3,2,1,0:T(8,128)S(1)}, f32[1,4,2,8,512]{4,3,2,1,0:T(8,128)}, u32[]{:S(2)}) copy-start(f32[1,4,2,8,512]{4,3,2,1,0:T(8,128)} %param.11) | copy-start | bytes 393220
  3.4 0.7 copy-start.3
  4.1 0.7 copy-start.4
  4.7 1.1 %copy-start.5 = (bf16[8,128,384]{2,1,0:T(8,128)(2,1)S(1)}, bf16[8,128,384]{2,1,0:T(8,128)(2,1)}, u32[]{:S(2)}) copy-start(bf16[8,128,384]{2,1,0:T(8,128)(2,1)} %constant.12.clone.e3_hbm) | copy-start | bytes 2359300
  5.9 1.1 %copy-start.6 = (bf16[8,192,256]{2,1,0:T(8,128)(2,1)S(1)}, bf16[8,192,256]{2,1,0:T(8,128)(2,1)}, u32[]{:S(2)}) copy-start(bf16[8,192,256]{2,1,0:T(8,128)(2,1)} %constant.11.clone.e2_hbm) | copy-start | bytes 2359300
  7.0 0.8 %copy-start.7 = (f32[128,128]{1,0:T(8,128)S(1)}, f32[128,128]{1,0:T(8,128)}, u32[]{:S(2)}) copy-start(f32[128,128]{1,0:T(8,128)} %constant.14.clone.coef) | copy-start | bytes 196612
where the time goes:
time: 75.9 us; the launch traced here: 75.5 us
  Pallas kernels  67 us (88%)
  local copies, waits for them, and re-layouts  8.5 us (11%)
    pallas_call x1, Pallas kernels, body(): pl.pallas_call(kernel, out_shape=jax.ShapeDtypeStruct((4, 2, 8, 512), F32...  67 us
    unnamed x17, local copies, waits for them, and re-layouts  8.5 us

commit v1 on v0

--- a/solution.py
+++ b/solution.py
@@ -34,7 +34,7 @@
 def tables():
     c, s = cos_sin(np.arange(512)[:, None] * np.arange(PAD)[None, :], PAD)
     w = np.concatenate([c.reshape(512, 4, 256), s.reshape(512, 4, 256)], axis=2).transpose(1, 0, 2)
-    w1 = np.stack(split_np(w))
+    w1 = np.stack(split_np(w), axis=1)
     r = 8 * np.arange(64)[None, :, None] + np.arange(8)[:, None, None]
     c, s = cos_sin(r * np.arange(128)[None, None, :], PAD)
     hi, lo = split_np(np.concatenate([c, s], axis=2))
@@ -44,12 +44,8 @@
     e3 = np.concatenate([hi, hi, lo], axis=2)
     c, s = cos_sin(np.arange(PAD)[:, None] * np.arange(512)[None, :], PAD)
     w = np.concatenate([c.reshape(PAD, 4, 128), s.reshape(PAD, 4, 128)], axis=2).transpose(1, 0, 2)
-    w4 = np.stack(split_np(w))
-    k = np.stack([2 * np.arange(4) + 2, 2 * np.arange(4) + 1], axis=1)
-    c, s = cos_sin(k[:, None, :] * np.arange(16)[None, :, None], SAMPLES)
-    co = np.stack([c, s]) * (2.0 / SAMPLES)
-    coef = np.repeat(co, 64, axis=3).astype(np.float32).reshape(128, 128)
-    return w1, e2, e3, w4, coef
+    w4 = np.stack(split_np(w), axis=1)
+    return w1, e2, e3, w4
 
 
 def dft8(z, sign):
@@ -103,14 +99,6 @@
     return v
 
 
-def halves(x, y):
-    left = lanes_of(x.shape) < 64
-    return (
-        jnp.where(left, x, pltpu.roll(y, 64, 1)),
-        jnp.where(left, pltpu.roll(x, 64, 1), y),
-    )
-
-
 def dot(a, b, ca=1, cb=0):
     return lax.dot_general(a, b, (((ca,), (cb,)), ((), ())), preferred_element_type=F32)
 
@@ -144,49 +132,141 @@
     pltpu.make_async_copy(src.at[rows], src.at[rows], send).wait()
 
 
+def greet(axis, count):
+    me = lax.axis_index(axis)
+
+    def step(i, carry):
+        pl.semaphore_signal(
+            pltpu.get_barrier_semaphore(),
+            inc=1,
+            device_id={axis: lax.rem(me + i, count)},
+            device_id_type=MESH,
+        )
+        return carry
+
+    lax.fori_loop(1, count, step, 0)
+
+
+def await_all(count):
+    pl.semaphore_wait(pltpu.get_barrier_semaphore(), count)
+
+
+def rows16(ref, i):
+    return ref.at[pl.ds(pl.multiple_of(16 * i, 16), 16), :]
+
+
+def pass_on(src, dst, to, harm, send, recv):
+    @pl.when(to != harm)
+    def _():
+        pltpu.make_async_remote_copy(
+            src_ref=src,
+            dst_ref=dst,
+            send_sem=send,
+            recv_sem=recv,
+            device_id={"harm": to},
+            device_id_type=MESH,
+        ).start()
+
+    @pl.when(to == harm)
+    def _():
+        dst[...] = src[...]
+
+
+def finish(count, src, dst, send, recv):
+    rows = pl.ds(0, count)
+    pltpu.make_async_copy(dst.at[rows], dst.at[rows], recv).wait()
+    pltpu.make_async_copy(src.at[rows], src.at[rows], send).wait()
+
+
+def trig(k, n):
+    angle = 2.0 * math.pi * ((k * n) % SAMPLES) / SAMPLES
+    return math.cos(angle), math.sin(angle)
+
+
+def waves(volts):
+    out = [None] * SAMPLES
+    for n in range(9):
+        sums = [None] * 4
+        for h in range(HARMS):
+            c, s = trig(h + 1, n)
+            for i, x in (((h + 1) % 2, volts[h][0] * c), (2 + (h + 1) % 2, volts[h][1] * s)):
+                sums[i] = x if sums[i] is None else sums[i] + x
+        ce, co, se, so = sums
+        p, m, u, v = ce + co, ce - co, se + so, se - so
+        out[n] = p - u
+        out[16 + n] = m - v
+        if n:
+            out[16 - n] = m + v
+            out[SAMPLES - n] = p + u
+    return out
+
+
+def harmonics(x, numbers):
+    sums = [[None, None] for _ in numbers]
+    odd = numbers[0] % 2
+    for n in range(9):
+        if n in (0, 8):
+            a, d = x[n], x[16 + n]
+            even, flat = (a - d, a - d) if odd else (a + d, a + d)
+        else:
+            a, b, c, d = x[n], x[SAMPLES - n], x[16 - n], x[16 + n]
+            even = (a + b) - (c + d) if odd else (a + b) + (c + d)
+            flat = (a - b) + (c - d) if odd else (a - b) - (c - d)
+        for i, k in enumerate(numbers):
+            for part, (y, w) in enumerate(zip((even, flat), trig(k, n))):
+                if abs(w) < 1e-12:
+                    continue
+                y = y * (w * 2.0 / SAMPLES)
+                sums[i][part] = y if sums[i][part] is None else sums[i][part] + y
+    return sums
+
+
 def kernel(
-    cur, inc, bias, coef, pw, g_hbm, w1_hbm, e2_hbm, e3_hbm, w4_hbm, out,
-    g, w1, e2, e3, w4, tx1, rx1, zb, yb, tx2, rx2, xk, tot, hs, hr, ds, dr, load, send, recv,
+    cur_hbm, inc_hbm, bias_hbm, pw_hbm, g_hbm, w1_hbm, e2_hbm, e3_hbm, w4_hbm, out,
+    cur, inc, bias, pw, g, w1, e2, e3, w4, tx1, rx1, zb, yb, tx2, rx2, xk, tot,
+    level, hs, hr, ds, dr, load, send, recv,
 ):
-    row, harm = lax.axis_index("row"), lax.axis_index("harm")
-    loads = [
-        pltpu.make_async_copy(a, b, load.at[i])
-        for i, (a, b) in enumerate(((w1_hbm, w1), (e2_hbm, e2), (g_hbm, g), (e3_hbm, e3), (w4_hbm, w4)))
-    ]
+    harm = lax.axis_index("harm")
+    x, zhi = harm // 2, lax.rem(harm, 2)
+    greet("harm", HARMS)
+    greet("row", NROW)
+    pairs = [(cur_hbm, cur)] + [(w1_hbm.at[j], w1.at[j]) for j in range(4)]
+    pairs += [(bias_hbm, bias), (pw_hbm, pw), (inc_hbm, inc), (e2_hbm, e2), (g_hbm, g), (e3_hbm, e3), (w4_hbm, w4)]
+    loads = [pltpu.make_async_copy(a, b, load.at[i]) for i, (a, b) in enumerate(pairs)]
     for c in loads:
         c.start()
-    barrier = pltpu.get_barrier_semaphore()
-
-    def greet(axis, me, count):
-        def step(i, carry):
-            pl.semaphore_signal(
-                barrier, inc=1, device_id={axis: lax.rem(me + i, count)}, device_id_type=MESH
-            )
-            return carry
-
-        lax.fori_loop(1, count, step, 0)
-
-    greet("harm", harm, HARMS)
-    greet("row", row, NROW)
 
     loads[0].wait()
     hi, lo = split(cur[...].reshape(64, 512))
     both = jnp.concatenate([hi, lo], axis=0)
     for j in range(4):
-        r1 = dot(both, w1[0, j])
-        r = r1[:64] + r1[64:] + dot(hi, w1[1, j])
+        loads[1 + j].wait()
+        r1 = dot(both, w1[j, 0])
+        r = r1[:64] + r1[64:] + dot(hi, w1[j, 1])
         r = r.reshape(4, 2, 8, 512)
         for half in range(2):
             c, s = r[..., 128 * half : 128 * half + 128], r[..., 256 + 128 * half : 384 + 128 * half]
             v = [c[b, 0] + s[b, 1] for b in range(4)] + [c[b, 1] - s[b, 0] for b in range(4)]
-            for i, x in enumerate(swap_blocks(v)):
+            for i, y in enumerate(swap_blocks(v)):
                 d = 16 * j + 8 * half + i
-                tx1[8 * d : 8 * d + 8, :] = x
-
-    pl.semaphore_wait(barrier, HARMS + NROW - 2)
+                tx1[8 * d : 8 * d + 8, :] = y
+    loads[5].wait()
+    own = bias[...].astype(F32)
+    level[0:8, :] = jnp.concatenate([own, own], axis=1)
+
+    await_all(HARMS + NROW - 2)
     spread("row", NROW, tx1, rx1, send.at[0], recv.at[0])
-    loads[1].wait()
-    loads[2].wait()
+    swap = pltpu.make_async_remote_copy(
+        src_ref=level.at[pl.ds(0, 8), :],
+        dst_ref=level.at[pl.ds(8, 8), :],
+        send_sem=send.at[4],
+        recv_sem=recv.at[4],
+        device_id={"harm": harm + 1 - 2 * zhi},
+        device_id_type=MESH,
+    )
+    swap.start()
+    for c in loads[6:]:
+        c.wait()
     settle(NROW, tx1, rx1, send.at[0], recv.at[0])
 
     def rows_forward(t, carry):
@@ -229,7 +309,6 @@
         return carry
 
     lax.fori_loop(0, 8, mix, 0)
-    loads[3].wait()
 
     def rows_inverse(t, carry):
         hi, lo = split(yb[t])
@@ -241,7 +320,6 @@
 
     lax.fori_loop(0, 8, rows_inverse, 0)
     spread("row", NROW, tx2, rx2, send.at[1], recv.at[1])
-    loads[4].wait()
     settle(NROW, tx2, rx2, send.at[1], recv.at[1])
 
     for j in range(8):
@@ -250,80 +328,75 @@
             xk[8 * i : 8 * i + 8, 128 * j : 128 * j + 128] = v[i]
     hi, lo = split(xk[...])
     both = jnp.concatenate([hi, lo], axis=0)
-    for u in range(4):
-        r1 = dot(both, w4[0, u])
-        r = r1[:64] + r1[64:] + dot(hi, w4[1, u])
+
+    def columns_inverse(i, carry):
+        u = lax.rem(x + 1 + i, 4)
+        r1 = dot(both, w4[u, 0])
+        r = r1[:64] + r1[64:] + dot(hi, w4[u, 1])
         fields = (r[:32, :128] - r[32:, 128:], r[32:, :128] + r[:32, 128:])
-        at = slice(128 * u, 128 * u + 128)
-        volt = []
+        at = pl.ds(pl.multiple_of(128 * u, 128), 128)
         for p in range(2):
             acc = None
             for b in range(4):
-                x = fields[p][8 * b : 8 * b + 8] + inc[b, p, :, at]
-                tot[b, p, :, at] = x
-                acc = pw[b] * x if b == 0 else acc + pw[b] * x
-            volt.append(acc)
-        hs[16 * u : 16 * u + 8, :], hs[16 * u + 8 : 16 * u + 16, :] = halves(*volt)
-
-    spread("harm", HARMS, hs, hr, send.at[2], recv.at[2])
-    settle(HARMS, hs, hr, send.at[2], recv.at[2])
-
+                y = fields[p][8 * b : 8 * b + 8] + inc[b, p, :, at]
+                tot[b, p, :, at] = y
+                acc = pw[b] * y if b == 0 else acc + pw[b] * y
+            hs[pl.ds(pl.multiple_of(16 * u + 8 * p, 8), 8), :] = acc
+        for z in range(2):
+            pass_on(rows16(hs, u), rows16(hr, harm), 2 * u + lax.rem(z + 1 + zhi, 2), harm, send.at[2], recv.at[2])
+        return carry
+
+    lax.fori_loop(0, 4, columns_inverse, 0)
+    swap.wait()
     left = lanes_of((8, 128)) < 64
-    sign = jnp.where(left, 1.0, -1.0)
-    volts = []
-    for h in range(HARMS):
-        v = hr[8 * h : 8 * h + 8, :]
-        w = pltpu.roll(v, 64, 1)
-        v0, v1 = jnp.where(left, v, w), jnp.where(left, w, v)
-        if h % 2 == 0:
-            v0, v1 = v0 * sign, v1 * sign
-        volts.append((v0, v1))
-    level = bias[...].astype(F32)
-    cap = 0.05 + 0.02 * jnp.concatenate([level, level], axis=1)
-    sums = [[None] * 4 for _ in range(4)]
-    for n in range(16):
-        wave = None
-        for h in range(HARMS):
-            angle = 2.0 * math.pi * (((h + 1) * n) % SAMPLES) / SAMPLES
-            x = volts[h][0] * math.cos(angle) - volts[h][1] * math.sin(angle)
-            wave = x if wave is None else wave + x
-        conduct = 0.05 * (jnp.exp(wave * 0.25) - 1.0)
-        charge = cap * (wave + 0.2 * wave * wave)
-        conduct = conduct * sign + pltpu.roll(conduct, 64, 1)
-        charge = charge * sign + pltpu.roll(charge, 64, 1)
-        for j in range(4):
-            cs = coef[16 * j + n : 16 * j + n + 1, :]
-            sn = coef[64 + 16 * j + n : 64 + 16 * j + n + 1, :]
-            terms = (conduct * cs, conduct * sn, charge * cs, charge * sn)
-            sums[j] = [t if a is None else a + t for a, t in zip(sums[j], terms)]
-    for j in range(4):
-        order = jnp.where(left, 0.25 * (2 * j + 2), 0.25 * (2 * j + 1))
-        cc, cn, qc, qn = sums[j]
-        even, odd = halves(cc + order * qn, order * qc - cn)
-        ds[16 * j : 16 * j + 8, :] = odd
-        ds[16 * j + 8 : 16 * j + 16, :] = even
-
-    spread("harm", HARMS, ds, dr, send.at[3], recv.at[3])
-    settle(HARMS, ds, dr, send.at[3], recv.at[3])
+    own, other = level[0:8, :], level[8:16, :]
+    cap = 0.05 + 0.02 * jnp.where(left == (zhi == 0), own, other)
+    finish(112, hr, hr, send.at[2], recv.at[2])
+
+    volts = [(hr[16 * h : 16 * h + 8, :], hr[16 * h + 8 : 16 * h + 16, :]) for h in range(HARMS)]
+    conduct, charge = [], []
+    for w in waves(volts):
+        conduct.append(0.05 * (jnp.exp(w * 0.25) - 1.0))
+        charge.append(cap * (w + 0.2 * w * w))
+    for z in range(2):
+
+        @pl.when(zhi == z)
+        def _():
+            numbers = [2 * i + z + 1 for i in range(4)]
+            for i, (k, (cc, cn), (qc, qn)) in enumerate(
+                zip(numbers, harmonics(conduct, numbers), harmonics(charge, numbers))
+            ):
+                ds[16 * i : 16 * i + 8, :] = cc + (0.25 * k) * qn
+                ds[16 * i + 8 : 16 * i + 16, :] = (0.25 * k) * qc - cn
+
+    def hand_back(i, carry):
+        to = lax.rem(x + 1 + i, 4)
+        pass_on(rows16(ds, to), rows16(dr, x), 2 * to + zhi, harm, send.at[3], recv.at[3])
+        return carry
+
+    lax.fori_loop(0, 4, hand_back, 0)
+    finish(48, ds, dr, send.at[3], recv.at[3])
     for u in range(4):
-        diode = halves(dr[16 * u : 16 * u + 8, :], dr[16 * u + 8 : 16 * u + 16, :])
         at = slice(128 * u, 128 * u + 128)
         for b in range(4):
             for p in range(2):
-                out[b, p, :, at] = tot[b, p, :, at] - pw[b] * diode[p]
+                out[b, p, :, at] = tot[b, p, :, at] - pw[b] * dr[16 * u + 8 * p : 16 * u + 8 * p + 8, :]
 
 
 def body(currents, incident, green, port_weights, bias_level):
-    w1, e2, e3, w4, coef = (jnp.asarray(t) for t in tables())
+    w1, e2, e3, w4 = (jnp.asarray(t) for t in tables())
     vmem = pl.BlockSpec(memory_space=pltpu.VMEM)
-    smem = pl.BlockSpec(memory_space=pltpu.SMEM)
     anyw = pl.BlockSpec(memory_space=pl.ANY)
     out = pl.pallas_call(
         kernel,
         out_shape=jax.ShapeDtypeStruct((4, 2, 8, 512), F32),
-        in_specs=[vmem, vmem, vmem, vmem, smem] + [anyw] * 5,
+        in_specs=[anyw] * 9,
         out_specs=vmem,
         scratch_shapes=[
+            pltpu.VMEM((4, 2, 8, 512), F32),
+            pltpu.VMEM((4, 2, 8, 512), F32),
+            pltpu.VMEM((8, 64), jnp.int32),
+            pltpu.SMEM((4,), F32),
             pltpu.VMEM((4, 4, 2, 16, 1024), F32),
             pltpu.VMEM(w1.shape, BF16),
             pltpu.VMEM(e2.shape, BF16),
@@ -337,19 +410,20 @@
             pltpu.VMEM((512, 128), F32),
             pltpu.VMEM((64, 1024), F32),
             pltpu.VMEM((4, 2, 8, 512), F32),
+            pltpu.VMEM((16, 128), F32),
+            pltpu.VMEM((64, 128), F32),
+            pltpu.VMEM((128, 128), F32),
             pltpu.VMEM((64, 128), F32),
             pltpu.VMEM((64, 128), F32),
-            pltpu.VMEM((64, 128), F32),
-            pltpu.VMEM((64, 128), F32),
+            pltpu.SemaphoreType.DMA((12,)),
             pltpu.SemaphoreType.DMA((5,)),
-            pltpu.SemaphoreType.DMA((4,)),
-            pltpu.SemaphoreType.DMA((4,)),
+            pltpu.SemaphoreType.DMA((5,)),
         ],
         compiler_params=pltpu.CompilerParams(
-            collective_id=0, has_side_effects=True, vmem_limit_bytes=48 * 2**20
+            collective_id=0, has_side_effects=True, vmem_limit_bytes=60 * 2**20
         ),
         cost_estimate=pl.CostEstimate(flops=5 * 10**9, bytes_accessed=13 * 10**6, transcendentals=16384),
-    )(currents[0], incident[0], bias_level, coef, port_weights, green[0], w1, e2, e3, w4)
+    )(currents[0], incident[0], bias_level, port_weights, green[0], w1, e2, e3, w4)
     return out[None]
 
 

time: 75.9 us -> 63.2 us (0.83)
  local copies, waits for them, and re-layouts: 8.5 us -> 1.57 us
  Pallas kernels: 67 us -> 61.5 us
    unnamed x17 -> x1, local copies, waits for them, and re-layouts: 8.5 us -> 1.57 us
    pallas_call x1, Pallas kernels: 67 us -> 61.5 us  [body(): pl.pallas_call(kernel, out_shape=jax.ShapeDtypeStruct((4, 2, 8, 512), F32...]
where the time goes in v1:
time: 63.2 us; the launch traced here: 63 us
  Pallas kernels  61.5 us (97%)
  local copies, waits for them, and re-layouts  1.57 us (2%)
    pallas_call x1, Pallas kernels, body(): pl.pallas_call(kernel, out_shape=jax.ShapeDtypeStruct((4, 2, 8, 512), F32...  61.5 us
    unnamed x1, local copies, waits for them, and re-layouts  1.57 us

profile of v1, /device:TPU:96, one launch (start us, length us, event | category | flops | bytes accessed | tf_op | source)
XLA Modules:
  0.0 63.0 jit_solution(14481194357153396250)
XLA Ops:
  0.0 61.5 %shard_map.91 = f32[4,2,8,512]{3,2,1,0:T(8,128)} custom-call(f32[4,2,8,512]{3,2,1,0:T(8,128)} %bitcast.6, f32[4,2,8,512]{3,2,1,0:T(8,128)} %bitcast.7, s32[8,64]{1,0:T(8,128)} %bias_hbm.1, f32[4]{0:T(128)} %pw_hbm.1, f32[4,4,2,16,1024]{4,3,2,1,0:T(8,128)} %bitcast.5, bf16[4,2,512,512]{3,2,1,0:T(8,128)(2,1)} %constant.8.clone.w1_hbm, ...), custom_call_target="tpu_custom_call" | custom-call | flops 5000000000 | bytes 13000000 | tf_op jit(solution)/shard_map/pallas_call | solution.py:390
  61.5 1.6 %copy.11 = f32[1,4,2,8,512]{4,3,2,1,0:T(8,128)} copy(f32[1,4,2,8,512]{4,3,2,1,0:T(8,128)} %bitcast.4) | data formatting | bytes 262144

commit v2 on v1

v2 whole, which is shorter than its diff:
```python
import functools
import math

import jax
import jax.numpy as jnp
import ml_dtypes
import numpy as np
from jax import lax
from jax.experimental import pallas as pl
from jax.experimental.pallas import tpu as pltpu
from jax.sharding import PartitionSpec as P

MESH = pl.DeviceIdType.MESH
F32 = jnp.float32
BF16 = jnp.bfloat16
HARMS = 8
SAMPLES = 32
NROW = 64
PAD = 1024


def split_np(table):
    high = table.astype(ml_dtypes.bfloat16)
    low = (table - high.astype(np.float64)).astype(ml_dtypes.bfloat16)
    return high, low


def cos_sin(product, length):
    angle = 2.0 * np.pi / length * (product % length).astype(np.float64)
    return np.cos(angle), np.sin(angle)


@functools.lru_cache(maxsize=None)
def tables():
    freq = np.arange(PAD).reshape(4, 16, 2, 8).transpose(0, 2, 1, 3).reshape(4, 2, 128)
    c, s = cos_sin(np.arange(512)[None, :, None] * freq.reshape(4, 1, 256), PAD)
    w1 = np.stack(split_np(np.concatenate([c, s], axis=2)), axis=1)
    r = 8 * np.arange(64)[None, :, None] + np.arange(4)[:, None, None]
    c, s = cos_sin(r * np.arange(128)[None, None, :], PAD)
    hi, lo = split_np(np.concatenate([c, s], axis=2))
    e2 = np.concatenate([hi, hi, lo], axis=1)
    hi, lo = split_np(np.concatenate([c, s], axis=1) / float(PAD * PAD))
    e3 = np.concatenate([hi, hi, lo], axis=2)
    freq = freq.transpose(1, 0, 2).reshape(2, 1, 512, 1)
    c, s = cos_sin(freq * np.arange(512).reshape(1, 4, 1, 128), PAD)
    w4 = np.stack(split_np(np.concatenate([c, s], axis=3)), axis=2)
    c, s = cos_sin(4 * np.arange(128), PAD)
    turn = np.zeros((8, 128), np.float32)
    turn[0], turn[1] = c, s
    return w1, e2, e3, w4, turn


def dft8(z, sign):
    def add(a, b):
        return (a[0] + b[0], a[1] + b[1])

    def sub(a, b):
        return (a[0] - b[0], a[1] - b[1])

    def turn(a):
        return (-a[1], a[0]) if sign > 0 else (a[1], -a[0])

    def four(a0, a1, a2, a3):
        p, m = add(a0, a2), sub(a0, a2)
        q, d = add(a1, a3), turn(sub(a1, a3))
        return [add(p, q), add(m, d), sub(p, q), sub(m, d)]

    even = four(z[0], z[2], z[4], z[6])
    odd = four(z[1], z[3], z[5], z[7])
    h = math.sqrt(0.5)
    o1, o3 = turn(odd[1]), turn(odd[3])
    odd = [
        odd[0],
        ((odd[1][0] + o1[0]) * h, (odd[1][1] + o1[1]) * h),
        turn(odd[2]),
        ((o3[0] - odd[3][0]) * h, (o3[1] - odd[3][1]) * h),
    ]
    return [add(e, o) for e, o in zip(even, odd)] + [sub(e, o) for e, o in zip(even, odd)]


def split(x):
    high = x.astype(BF16)
    return high, (x - high.astype(F32)).astype(BF16)


def lanes_of(shape):
    return lax.broadcasted_iota(jnp.int32, shape, 1)


def swap_blocks(v):
    lane = lanes_of((8, 128))
    stay = (lax.broadcasted_iota(jnp.int32, (8, 128), 0) < 4) == (lane < 64)
    v = [jnp.where(stay, x, pltpu.roll(pltpu.roll(x, 4, 0), 64, 1)) for x in v]
    for bit in (4, 2, 1):
        shift = 8 * bit
        keep = (lane & shift) == 0
        for a in range(8):
            if a & bit:
                continue
            x, y = v[a], v[a + bit]
            v[a] = jnp.where(keep, x, pltpu.roll(y, shift, 1))
            v[a + bit] = jnp.where(keep, pltpu.roll(x, 128 - shift, 1), y)
    return v


def dot(a, b, ca=1, cb=0):
    return lax.dot_general(a, b, (((ca,), (cb,)), ((), ())), preferred_element_type=F32)


def slot(d):
    return 64 * (d // 16) + 8 * lax.rem(d, 8) + 4 * lax.rem(d // 8, 2)


def ordered(d):
    return 4 * d


def rows4(ref, half, at):
    return ref.at[pl.ds(pl.multiple_of(256 * half + at, 4), 4), :]


def spread(half, src, from_slot, dst, to_slot, send, recv):
    me = lax.axis_index("row")
    here = to_slot(me)

    def step(i, carry):
        to = lax.rem(me + i, NROW)
        pltpu.make_async_remote_copy(
            src_ref=rows4(src, half, from_slot(to)),
            dst_ref=rows4(dst, half, here),
            send_sem=send,
            recv_sem=recv,
            device_id={"row": to},
            device_id_type=MESH,
        ).start()
        return carry

    lax.fori_loop(1, NROW, step, 0)
    rows4(dst, half, here)[...] = rows4(src, half, from_slot(me))[...]


def settle(ref, count, sem):
    rows = pl.ds(0, count)
    pltpu.make_async_copy(ref.at[rows], ref.at[rows], sem).wait()


def greet(axis, count):
    me = lax.axis_index(axis)

    def step(i, carry):
        pl.semaphore_signal(
            pltpu.get_barrier_semaphore(),
            inc=1,
            device_id={axis: lax.rem(me + i, count)},
            device_id_type=MESH,
        )
        return carry

    lax.fori_loop(1, count, step, 0)


def await_all(count):
    pl.semaphore_wait(pltpu.get_barrier_semaphore(), count)


def rows16(ref, i):
    return ref.at[pl.ds(pl.multiple_of(16 * i, 16), 16), :]


def pass_on(src, dst, to, harm, send, recv):
    @pl.when(to != harm)
    def _():
        pltpu.make_async_remote_copy(
            src_ref=src,
            dst_ref=dst,
            send_sem=send,
            recv_sem=recv,
            device_id={"harm": to},
            device_id_type=MESH,
        ).start()

    @pl.when(to == harm)
    def _():
        dst[...] = src[...]


def trig(k, n):
    angle = 2.0 * math.pi * ((k * n) % SAMPLES) / SAMPLES
    return math.cos(angle), math.sin(angle)


def waves(volts):
    out = [None] * SAMPLES
    for n in range(9):
        sums = [None] * 4
        for h in range(HARMS):
            c, s = trig(h + 1, n)
            for i, x in (((h + 1) % 2, volts[h][0] * c), (2 + (h + 1) % 2, volts[h][1] * s)):
                sums[i] = x if sums[i] is None else sums[i] + x
        ce, co, se, so = sums
        p, m, u, v = ce + co, ce - co, se + so, se - so
        out[n] = p - u
        out[16 + n] = m - v
        if n:
            out[16 - n] = m + v
            out[SAMPLES - n] = p + u
    return out


def harmonics(x, numbers):
    sums = [[None, None] for _ in numbers]
    odd = numbers[0] % 2
    for n in range(9):
        if n in (0, 8):
            a, d = x[n], x[16 + n]
            even, flat = (a - d, a - d) if odd else (a + d, a + d)
        else:
            a, b, c, d = x[n], x[SAMPLES - n], x[16 - n], x[16 + n]
            even = (a + b) - (c + d) if odd else (a + b) + (c + d)
            flat = (a - b) + (c - d) if odd else (a - b) - (c - d)
        for i, k in enumerate(numbers):
            for part, (y, w) in enumerate(zip((even, flat), trig(k, n))):
                if abs(w) < 1e-12:
                    continue
                y = y * (w * 2.0 / SAMPLES)
                sums[i][part] = y if sums[i][part] is None else sums[i][part] + y
    return sums


def kernel(
    cur_hbm, inc_hbm, bias_hbm, pw_hbm, turn_hbm, g_hbm, w1_hbm, e2_hbm, e3_hbm, w4_hbm, out,
    cur, inc, bias, pw, turn, g, w1, e2, e3, w4, tx1, rx1, zb, yb, tx2, rx2, xk, part, tot,
    level, hs, hr, ds, dr, load, send, recv,
):
    harm = lax.axis_index("harm")
    x, zhi = harm // 2, lax.rem(harm, 2)
    greet("harm", HARMS)
    greet("row", NROW)
    pairs = [(cur_hbm, cur)] + [(w1_hbm.at[j], w1.at[j]) for j in range(4)]
    pairs += [(bias_hbm, bias), (pw_hbm, pw), (turn_hbm, turn), (e2_hbm, e2), (g_hbm, g), (e3_hbm, e3)]
    pairs += [(inc_hbm, inc), (w4_hbm, w4)]
    loads = [pltpu.make_async_copy(a, b, load.at[i]) for i, (a, b) in enumerate(pairs)]
    for c in loads:
        c.start()

    loads[0].wait()
    hi, lo = split(cur[...].reshape(64, 512))
    both = jnp.concatenate([hi, lo], axis=0)
    for j in range(4):
        loads[1 + j].wait()
        r1 = dot(both, w1[j, 0])
        r = r1[:64] + r1[64:] + dot(hi, w1[j, 1])
        r = r.reshape(4, 2, 8, 512)
        for half in range(2):
            c, s = r[..., 128 * half : 128 * half + 128], r[..., 256 + 128 * half : 384 + 128 * half]
            v = [c[b, 0] + s[b, 1] for b in range(4)] + [c[b, 1] - s[b, 0] for b in range(4)]
            for i, y in enumerate(swap_blocks(v)):
                at = 256 * half + 64 * j + 8 * i
                tx1[at : at + 8, :] = y
    loads[5].wait()
    own = bias[...].astype(F32)
    level[0:8, :] = jnp.concatenate([own, own], axis=1)

    await_all(HARMS + NROW - 2)
    for half in range(2):
        spread(half, tx1, slot, rx1, ordered, send.at[half], recv.at[half])
    swap = pltpu.make_async_remote_copy(
        src_ref=level.at[pl.ds(0, 8), :],
        dst_ref=level.at[pl.ds(8, 8), :],
        send_sem=send.at[6],
        recv_sem=recv.at[6],
        device_id={"harm": harm + 1 - 2 * zhi},
        device_id_type=MESH,
    )
    swap.start()
    for c in loads[6:11]:
        c.wait()
    tc, ts = turn[0:1, :], turn[1:2, :]
    inner = (lanes_of((64, 128)) & 32) == 0

    for half in range(2):
        settle(rx1, 252, recv.at[half])
        for t in range(4):
            hi, lo = split(rx1[pl.ds(256 * half + t, 64, stride=4), :])
            r = dot(jnp.concatenate([hi, lo, hi], axis=0), e2[t], 0, 0)
            p, q = r[:, :128], r[:, 128:]
            zb[t, 0], zb[t, 1] = p[:32] + q[32:64], p[32:64] - q[:32]
            re, im = p[64:96] + q[96:], p[96:] - q[64:96]
            zb[4 + t, 0], zb[4 + t, 1] = re * tc + im * ts, im * tc - re * ts
        for c in range(4):
            at = slice(8 * c, 8 * c + 8)
            z = dft8([(zb[t, 0, at, :], zb[t, 1, at, :]) for t in range(8)], -1)
            for q in range(8):
                zb[q, 0, at, :], zb[q, 1, at, :] = z[q]

        def mix(b, carry):
            f = []
            for q in range(8):
                re = im = None
                for c in range(4):
                    sr, si = zb[q, 0, 8 * c : 8 * c + 8, :], zb[q, 1, 8 * c : 8 * c + 8, :]
                    gr, gi = (
                        g[b, c, p, 8 * half : 8 * half + 8, 128 * q : 128 * q + 128] for p in range(2)
                    )
                    u, w = gr * sr - gi * si, gr * si + gi * sr
                    re, im = (u, w) if c == 0 else (re + u, im + w)
                f.append((re, im))
            y = dft8(f, 1)
            for t in range(4):
                (ar, ai), (br, bi) = y[t], y[4 + t]
                for p, w in enumerate((ar, ai, br * tc - bi * ts, bi * tc + br * ts)):
                    yb[t, pl.ds(pl.multiple_of(32 * p + 8 * b, 8), 8), :] = w
            return carry

        lax.fori_loop(0, 4, mix, 0)
        for t in range(4):
            hi, lo = split(yb[t])
            r = dot(e3[t], jnp.concatenate([hi, lo, hi], axis=1), 1, 1)
            s = r[64:]
            turned = jnp.where(inner, -pltpu.roll(s, 96, 1), pltpu.roll(s, 32, 1))
            tx2[pl.ds(256 * half + t, 64, stride=4), :] = r[:64] + turned
        spread(half, tx2, ordered, rx2, slot, send.at[2 + half], recv.at[2 + half])

    for c in loads[11:]:
        c.wait()
    for half in range(2):
        settle(rx2, 252, recv.at[2 + half])
        for j in range(4):
            at = 256 * half + 64 * j
            v = swap_blocks([rx2[at + 8 * i : at + 8 * i + 8, :] for i in range(8)])
            for i in range(8):
                xk[8 * i : 8 * i + 8, 128 * j : 128 * j + 128] = v[i]
        hi, lo = split(xk[...])
        both = jnp.concatenate([hi, lo], axis=0)
        if half == 0:
            for u in range(4):
                r1 = dot(both, w4[0, u, 0])
                part[u] = r1[:64] + r1[64:] + dot(hi, w4[0, u, 1])

    def columns_inverse(i, carry):
        u = lax.rem(x + 1 + i, 4)
        r1 = dot(both, w4[1, u, 0])
        r = r1[:64] + r1[64:] + dot(hi, w4[1, u, 1]) + part[u]
        fields = (r[:32, :128] - r[32:, 128:], r[32:, :128] + r[:32, 128:])
        at = pl.ds(pl.multiple_of(128 * u, 128), 128)
        for p in range(2):
            acc = None
            for b in range(4):
                y = fields[p][8 * b : 8 * b + 8] + inc[b, p, :, at]
                tot[b, p, :, at] = y
                acc = pw[b] * y if b == 0 else acc + pw[b] * y
            hs[pl.ds(pl.multiple_of(16 * u + 8 * p, 8), 8), :] = acc
        for z in range(2):
            pass_on(rows16(hs, u), rows16(hr, harm), 2 * u + lax.rem(z + 1 + zhi, 2), harm, send.at[4], recv.at[4])
        return carry

    lax.fori_loop(0, 4, columns_inverse, 0)
    swap.wait()
    left = lanes_of((8, 128)) < 64
    own, other = level[0:8, :], level[8:16, :]
    cap = 0.05 + 0.02 * jnp.where(left == (zhi == 0), own, other)
    settle(hr, 112, recv.at[4])

    volts = [(hr[16 * h : 16 * h + 8, :], hr[16 * h + 8 : 16 * h + 16, :]) for h in range(HARMS)]
    conduct, charge = [], []
    for w in waves(volts):
        conduct.append(0.05 * (jnp.exp(w * 0.25) - 1.0))
        charge.append(cap * (w + 0.2 * w * w))
    for z in range(2):

        @pl.when(zhi == z)
        def _():
            numbers = [2 * i + z + 1 for i in range(4)]
            for i, (k, (cc, cn), (qc, qn)) in enumerate(
                zip(numbers, harmonics(conduct, numbers), harmonics(charge, numbers))
            ):
                ds[16 * i : 16 * i + 8, :] = cc + (0.25 * k) * qn
                ds[16 * i + 8 : 16 * i + 16, :] = (0.25 * k) * qc - cn

    def hand_back(i, carry):
        to = lax.rem(x + 1 + i, 4)
        pass_on(rows16(ds, to), rows16(dr, x), 2 * to + zhi, harm, send.at[5], recv.at[5])
        return carry

    lax.fori_loop(0, 4, hand_back, 0)
    settle(dr, 48, recv.at[5])
    for u in range(4):
        at = slice(128 * u, 128 * u + 128)
        for b in range(4):
            for p in range(2):
                out[b, p, :, at] = tot[b, p, :, at] - pw[b] * dr[16 * u + 8 * p : 16 * u + 8 * p + 8, :]
    for i in range(4):
        settle((tx1, tx1, tx2, tx2)[i], 252, send.at[i])
    settle(hr, 112, send.at[4])
    settle(ds, 48, send.at[5])


def body(currents, incident, green, port_weights, bias_level):
    w1, e2, e3, w4, turn = (jnp.asarray(t) for t in tables())
    vmem = pl.BlockSpec(memory_space=pltpu.VMEM)
    anyw = pl.BlockSpec(memory_space=pltpu.HBM)
    out = pl.pallas_call(
        kernel,
        out_shape=jax.ShapeDtypeStruct((4, 2, 8, 512), F32),
        in_specs=[anyw] * 10,
        out_specs=vmem,
        scratch_shapes=[
            pltpu.VMEM((4, 2, 8, 512), F32),
            pltpu.VMEM((4, 2, 8, 512), F32),
            pltpu.VMEM((8, 64), jnp.int32),
            pltpu.SMEM((4,), F32),
            pltpu.VMEM((8, 128), F32),
            pltpu.VMEM((4, 4, 2, 16, 1024), F32),
            pltpu.VMEM(w1.shape, BF16),
            pltpu.VMEM(e2.shape, BF16),
            pltpu.VMEM(e3.shape, BF16),
            pltpu.VMEM(w4.shape, BF16),
            pltpu.VMEM((512, 128), F32),
            pltpu.VMEM((512, 128), F32),
            pltpu.VMEM((8, 2, 32, 128), F32),
            pltpu.VMEM((4, 128, 128), F32),
            pltpu.VMEM((512, 128), F32),
            pltpu.VMEM((512, 128), F32),
            pltpu.VMEM((64, 512), F32),
            pltpu.VMEM((4, 64, 256), F32),
            pltpu.VMEM((4, 2, 8, 512), F32),
            pltpu.VMEM((16, 128), F32),
            pltpu.VMEM((64, 128), F32),
            pltpu.VMEM((128, 128), F32),
            pltpu.VMEM((64, 128), F32),
            pltpu.VMEM((64, 128), F32),
            pltpu.SemaphoreType.DMA((13,)),
            pltpu.SemaphoreType.DMA((7,)),
            pltpu.SemaphoreType.DMA((7,)),
        ],
        compiler_params=pltpu.CompilerParams(
            collective_id=0, has_side_effects=True, vmem_limit_bytes=60 * 2**20
        ),
        cost_estimate=pl.CostEstimate(flops=5 * 10**9, bytes_accessed=13 * 10**6, transcendentals=16384),
    )(currents[0], incident[0], bias_level, port_weights, turn, green[0], w1, e2, e3, w4)
    return out[None]


def solution(mesh):
    placed = (
        P("harm", None, None, "row", None),
        P("harm", None, None, "row", None),
        P("harm", None, None, None, "row", None),
        P(),
        P("row", "harm"),
    )
    return jax.shard_map(
        body,
        mesh=mesh,
        in_specs=placed,
        out_specs=P("harm", None, None, "row", None),
        check_vma=False,
    )
```

time: 63.2 us -> 58.8 us (0.930)
  the two profiles are of different devices: /device:TPU:96 before, /device:TPU:1 now
where the time goes in v2:
time: 58.8 us; the launch traced here: 58.6 us
  Pallas kernels  57 us (97%)
  local copies, waits for them, and re-layouts  1.57 us (3%)
    pallas_call x1, Pallas kernels, body(): pl.pallas_call(kernel, out_shape=jax.ShapeDtypeStruct((4, 2, 8, 512), F32...  57 us
    unnamed x1, local copies, waits for them, and re-layouts  1.57 us

profile of v2, /device:TPU:1, one launch (start us, length us, event | category | flops | bytes accessed | tf_op | source)
XLA Modules:
  0.0 58.6 jit_solution(6252808903079407770)
XLA Ops:
  0.0 57.0 %shard_map.100 = f32[4,2,8,512]{3,2,1,0:T(8,128)} custom-call(f32[4,2,8,512]{3,2,1,0:T(8,128)} %bitcast.6, f32[4,2,8,512]{3,2,1,0:T(8,128)} %bitcast.7, s32[8,64]{1,0:T(8,128)} %bias_hbm.1, f32[4]{0:T(128)} %pw_hbm.1, f32[8,128]{1,0:T(8,128)} %constant.14.clone.turn_hbm, f32[4,4,2,16,1024]{4,3,2,1,0:T(8,128)} %bitcast.5, ...), custom_call_target="tpu_custom_call" | custom-call | flops 5000000000 | bytes 13000000 | tf_op jit(solution)/shard_map/pallas_call | solution.py:402
  57.0 1.6 %copy.12 = f32[1,4,2,8,512]{4,3,2,1,0:T(8,128)} copy(f32[1,4,2,8,512]{4,3,2,1,0:T(8,128)} %bitcast.4) | data formatting | bytes 262144

commit v3 on v2

--- a/solution.py
+++ b/solution.py
@@ -39,14 +39,13 @@
     c, s = cos_sin(r * np.arange(128)[None, None, :], PAD)
     hi, lo = split_np(np.concatenate([c, s], axis=2))
     e2 = np.concatenate([hi, hi, lo], axis=1)
-    hi, lo = split_np(np.concatenate([c, s], axis=1) / float(PAD * PAD))
-    e3 = np.concatenate([hi, hi, lo], axis=2)
-    freq = freq.transpose(1, 0, 2).reshape(2, 1, 512, 1)
+    c, s = cos_sin(8 * np.arange(64)[:, None] * np.arange(128)[None, :], PAD)
+    hi, lo = split_np(np.concatenate([c, s], axis=0) / float(PAD * PAD))
+    e3 = np.concatenate([hi, hi, lo], axis=1)
+    freq = np.arange(PAD).reshape(64, 2, 8).transpose(1, 2, 0).reshape(2, 1, 512, 1)
     c, s = cos_sin(freq * np.arange(512).reshape(1, 4, 1, 128), PAD)
     w4 = np.stack(split_np(np.concatenate([c, s], axis=3)), axis=2)
-    c, s = cos_sin(4 * np.arange(128), PAD)
-    turn = np.zeros((8, 128), np.float32)
-    turn[0], turn[1] = c, s
+    turn = np.concatenate(cos_sin(np.arange(8)[:, None] * np.arange(128)[None, :], PAD)).astype(np.float32)
     return w1, e2, e3, w4, turn
 
 
@@ -103,31 +102,46 @@
     return v
 
 
+def to_rows(x, y, ref):
+    ref[...] = jnp.concatenate([x, y], axis=0).T
+    left = lanes_of((16, 128)) < 64
+    first, second = [], []
+    for i in range(4):
+        p, q = (ref[pl.ds(2 * i + j, 16, stride=8), :] for j in range(2))
+        first.append(jnp.where(left, p, pltpu.roll(q, 64, 1)))
+        second.append(jnp.where(left, pltpu.roll(p, 64, 1), q))
+    return jnp.concatenate(first, axis=1), jnp.concatenate(second, axis=1)
+
+
+def to_columns(x, w, u):
+    hi, lo = split(x)
+    rows = x.shape[0]
+    r = dot(jnp.concatenate([hi, lo], axis=0), w[u, 0])
+    return r[:rows] + r[rows:] + dot(hi, w[u, 1])
+
+
+def parts(r):
+    return r[:8, :128] - r[8:, 128:], r[8:, :128] + r[:8, 128:]
+
+
 def dot(a, b, ca=1, cb=0):
     return lax.dot_general(a, b, (((ca,), (cb,)), ((), ())), preferred_element_type=F32)
 
 
-def slot(d):
-    return 64 * (d // 16) + 8 * lax.rem(d, 8) + 4 * lax.rem(d // 8, 2)
-
-
-def ordered(d):
-    return 4 * d
-
-
-def rows4(ref, half, at):
-    return ref.at[pl.ds(pl.multiple_of(256 * half + at, 4), 4), :]
-
-
-def spread(half, src, from_slot, dst, to_slot, send, recv):
+def rows_at(ref, count, at):
+    if count > 1:
+        at = pl.multiple_of(at, 2 if count == 2 else 8)
+    return ref.at[pl.ds(at, count), :]
+
+
+def spread(count, src, place, dst, here, send, recv):
     me = lax.axis_index("row")
-    here = to_slot(me)
 
     def step(i, carry):
         to = lax.rem(me + i, NROW)
         pltpu.make_async_remote_copy(
-            src_ref=rows4(src, half, from_slot(to)),
-            dst_ref=rows4(dst, half, here),
+            src_ref=rows_at(src, count, place(to)),
+            dst_ref=rows_at(dst, count, here),
             send_sem=send,
             recv_sem=recv,
             device_id={"row": to},
@@ -136,7 +150,7 @@
         return carry
 
     lax.fori_loop(1, NROW, step, 0)
-    rows4(dst, half, here)[...] = rows4(src, half, from_slot(me))[...]
+    rows_at(dst, count, here)[...] = rows_at(src, count, place(me))[...]
 
 
 def settle(ref, count, sem):
@@ -151,7 +165,7 @@
         pl.semaphore_signal(
             pltpu.get_barrier_semaphore(),
             inc=1,
-            device_id={axis: lax.rem(me + i, count)},
+            device_id={axis: me ^ (count - i)},
             device_id_type=MESH,
         )
         return carry
@@ -229,7 +243,7 @@
 
 def kernel(
     cur_hbm, inc_hbm, bias_hbm, pw_hbm, turn_hbm, g_hbm, w1_hbm, e2_hbm, e3_hbm, w4_hbm, out,
-    cur, inc, bias, pw, turn, g, w1, e2, e3, w4, tx1, rx1, zb, yb, tx2, rx2, xk, part, tot,
+    cur, inc, bias, pw, turn, g, w1, e2, e3, w4, tx1, rx1, zb, yb, txv, rxv, txr, rxr, tr, vinc, vf, ff,
     level, hs, hr, ds, dr, load, send, recv,
 ):
     harm = lax.axis_index("harm")
@@ -255,45 +269,63 @@
             c, s = r[..., 128 * half : 128 * half + 128], r[..., 256 + 128 * half : 384 + 128 * half]
             v = [c[b, 0] + s[b, 1] for b in range(4)] + [c[b, 1] - s[b, 0] for b in range(4)]
             for i, y in enumerate(swap_blocks(v)):
-                at = 256 * half + 64 * j + 8 * i
-                tx1[at : at + 8, :] = y
+                at = 8 * (16 * j + i) + 4 * half
+                tx1[at : at + 4, :] = y[:4]
+                tx1[at + 64 : at + 68, :] = y[4:]
     loads[5].wait()
     own = bias[...].astype(F32)
     level[0:8, :] = jnp.concatenate([own, own], axis=1)
 
+    row = lax.axis_index("row")
     await_all(HARMS + NROW - 2)
-    for half in range(2):
-        spread(half, tx1, slot, rx1, ordered, send.at[half], recv.at[half])
+    spread(8, tx1, lambda d: 8 * d, rx1, 8 * row, send.at[0], recv.at[0])
     swap = pltpu.make_async_remote_copy(
         src_ref=level.at[pl.ds(0, 8), :],
         dst_ref=level.at[pl.ds(8, 8), :],
-        send_sem=send.at[6],
-        recv_sem=recv.at[6],
+        send_sem=send.at[5],
+        recv_sem=recv.at[5],
         device_id={"harm": harm + 1 - 2 * zhi},
         device_id_type=MESH,
     )
     swap.start()
-    for c in loads[6:11]:
+    for c in loads[6:]:
         c.wait()
-    tc, ts = turn[0:1, :], turn[1:2, :]
-    inner = (lanes_of((64, 128)) & 32) == 0
-
+    for p in range(2):
+        vinc[p] = pw[0] * inc[0, p] + pw[1] * inc[1, p] + pw[2] * inc[2, p] + pw[3] * inc[3, p]
+    tc = [turn[t : t + 1, :] for t in range(8)]
+    ts = [turn[8 + t : 9 + t, :] for t in range(8)]
+    left = lanes_of((64, 128)) < 64
+
+    def rows_inverse(i):
+        hi, lo = split(yb[i])
+        r = dot(e3[...], jnp.concatenate([hi, lo, hi], axis=1), 1, 1)
+        s = pltpu.roll(r[64:], 64, 1)
+        return r[:64] + jnp.where(left, -s, s)
+
+    settle(rx1, 504, recv.at[0])
     for half in range(2):
-        settle(rx1, 252, recv.at[half])
         for t in range(4):
-            hi, lo = split(rx1[pl.ds(256 * half + t, 64, stride=4), :])
+            hi, lo = split(rx1[pl.ds(4 * half + t, 64, stride=8), :])
             r = dot(jnp.concatenate([hi, lo, hi], axis=0), e2[t], 0, 0)
             p, q = r[:, :128], r[:, 128:]
             zb[t, 0], zb[t, 1] = p[:32] + q[32:64], p[32:64] - q[:32]
             re, im = p[64:96] + q[96:], p[96:] - q[64:96]
-            zb[4 + t, 0], zb[4 + t, 1] = re * tc + im * ts, im * tc - re * ts
+            zb[4 + t, 0], zb[4 + t, 1] = re * tc[4] + im * ts[4], im * tc[4] - re * ts[4]
         for c in range(4):
             at = slice(8 * c, 8 * c + 8)
             z = dft8([(zb[t, 0, at, :], zb[t, 1, at, :]) for t in range(8)], -1)
             for q in range(8):
                 zb[q, 0, at, :], zb[q, 1, at, :] = z[q]
 
-        def mix(b, carry):
+        def keep(i, f):
+            for t, (re, im) in enumerate(dft8(f, 1)):
+                if t:
+                    re, im = re * tc[t] - im * ts[t], im * tc[t] + re * ts[t]
+                yb[4 * half + i, 8 * t : 8 * t + 8, :] = re
+                yb[4 * half + i, 64 + 8 * t : 72 + 8 * t, :] = im
+
+        port = None
+        for b in range(4):
             f = []
             for q in range(8):
                 re = im = None
@@ -305,61 +337,45 @@
                     u, w = gr * sr - gi * si, gr * si + gi * sr
                     re, im = (u, w) if c == 0 else (re + u, im + w)
                 f.append((re, im))
-            y = dft8(f, 1)
-            for t in range(4):
-                (ar, ai), (br, bi) = y[t], y[4 + t]
-                for p, w in enumerate((ar, ai, br * tc - bi * ts, bi * tc + br * ts)):
-                    yb[t, pl.ds(pl.multiple_of(32 * p + 8 * b, 8), 8), :] = w
-            return carry
-
-        lax.fori_loop(0, 4, mix, 0)
-        for t in range(4):
-            hi, lo = split(yb[t])
-            r = dot(e3[t], jnp.concatenate([hi, lo, hi], axis=1), 1, 1)
-            s = r[64:]
-            turned = jnp.where(inner, -pltpu.roll(s, 96, 1), pltpu.roll(s, 32, 1))
-            tx2[pl.ds(256 * half + t, 64, stride=4), :] = r[:64] + turned
-        spread(half, tx2, ordered, rx2, slot, send.at[2 + half], recv.at[2 + half])
-
-    for c in loads[11:]:
-        c.wait()
+            if b < 3:
+                keep(b + 1, f)
+            terms = [(pw[b] * re, pw[b] * im) for re, im in f]
+            port = terms if b == 0 else [(v[0] + w[0], v[1] + w[1]) for v, w in zip(port, terms)]
+        keep(0, port)
+        txv[pl.ds(half, 64, stride=2), :] = rows_inverse(4 * half)
+    spread(2, txv, lambda d: 2 * d, rxv, 2 * row, send.at[1], recv.at[1])
     for half in range(2):
-        settle(rx2, 252, recv.at[2 + half])
-        for j in range(4):
-            at = 256 * half + 64 * j
-            v = swap_blocks([rx2[at + 8 * i : at + 8 * i + 8, :] for i in range(8)])
-            for i in range(8):
-                xk[8 * i : 8 * i + 8, 128 * j : 128 * j + 128] = v[i]
-        hi, lo = split(xk[...])
-        both = jnp.concatenate([hi, lo], axis=0)
-        if half == 0:
-            for u in range(4):
-                r1 = dot(both, w4[0, u, 0])
-                part[u] = r1[:64] + r1[64:] + dot(hi, w4[0, u, 1])
-
-    def columns_inverse(i, carry):
+        for i in range(3):
+            txr[pl.ds(3 * half + i, 64, stride=8), :] = rows_inverse(4 * half + 1 + i)
+    spread(6, txr, lambda d: 8 * d, rxr, 8 * row, send.at[2], recv.at[2])
+
+    def block(i, half):
+        return rxr[pl.ds(3 * half + i, 64, stride=8), :]
+
+    settle(rxv, 126, recv.at[1])
+    x0, x1 = to_rows(*(rxv[pl.ds(half, 64, stride=2), :] for half in range(2)), tr.at[0])
+    for i in range(4):
         u = lax.rem(x + 1 + i, 4)
-        r1 = dot(both, w4[1, u, 0])
-        r = r1[:64] + r1[64:] + dot(hi, w4[1, u, 1]) + part[u]
-        fields = (r[:32, :128] - r[32:, 128:], r[32:, :128] + r[:32, 128:])
         at = pl.ds(pl.multiple_of(128 * u, 128), 128)
-        for p in range(2):
-            acc = None
-            for b in range(4):
-                y = fields[p][8 * b : 8 * b + 8] + inc[b, p, :, at]
-                tot[b, p, :, at] = y
-                acc = pw[b] * y if b == 0 else acc + pw[b] * y
-            hs[pl.ds(pl.multiple_of(16 * u + 8 * p, 8), 8), :] = acc
+        for p, y in enumerate(parts(to_columns(x0, w4.at[0], u) + to_columns(x1, w4.at[1], u))):
+            vf[p, :, at] = y
+            hs[pl.ds(pl.multiple_of(16 * u + 8 * p, 8), 8), :] = y + vinc[p, :, at]
         for z in range(2):
-            pass_on(rows16(hs, u), rows16(hr, harm), 2 * u + lax.rem(z + 1 + zhi, 2), harm, send.at[4], recv.at[4])
-        return carry
-
-    lax.fori_loop(0, 4, columns_inverse, 0)
+            pass_on(rows16(hs, u), rows16(hr, harm), 2 * u + lax.rem(z + 1 + zhi, 2), harm, send.at[3], recv.at[3])
+
+    settle(rxr, 378, recv.at[2])
+    both = [to_rows(block(i, 0), block(i, 1), tr.at[1 + i]) for i in range(3)]
+    xa = [jnp.concatenate([both[i][half] for i in range(3)], axis=0) for half in range(2)]
+    for u in range(4):
+        r = to_columns(xa[0], w4.at[0], u) + to_columns(xa[1], w4.at[1], u)
+        for i in range(3):
+            for p, y in enumerate(parts(r[16 * i : 16 * i + 16])):
+                ff[i, p, :, 128 * u : 128 * u + 128] = y
     swap.wait()
     left = lanes_of((8, 128)) < 64
     own, other = level[0:8, :], level[8:16, :]
     cap = 0.05 + 0.02 * jnp.where(left == (zhi == 0), own, other)
-    settle(hr, 112, recv.at[4])
+    settle(hr, 112, recv.at[3])
 
     volts = [(hr[16 * h : 16 * h + 8, :], hr[16 * h + 8 : 16 * h + 16, :]) for h in range(HARMS)]
     conduct, charge = [], []
@@ -379,20 +395,27 @@
 
     def hand_back(i, carry):
         to = lax.rem(x + 1 + i, 4)
-        pass_on(rows16(ds, to), rows16(dr, x), 2 * to + zhi, harm, send.at[5], recv.at[5])
+        pass_on(rows16(ds, to), rows16(dr, x), 2 * to + zhi, harm, send.at[4], recv.at[4])
         return carry
 
     lax.fori_loop(0, 4, hand_back, 0)
-    settle(dr, 48, recv.at[5])
+
+    last = 1.0 / jnp.full((8, 128), pw[3], F32)
+    settle(dr, 48, recv.at[4])
     for u in range(4):
         at = slice(128 * u, 128 * u + 128)
-        for b in range(4):
-            for p in range(2):
-                out[b, p, :, at] = tot[b, p, :, at] - pw[b] * dr[16 * u + 8 * p : 16 * u + 8 * p + 8, :]
-    for i in range(4):
-        settle((tx1, tx1, tx2, tx2)[i], 252, send.at[i])
-    settle(hr, 112, send.at[4])
-    settle(ds, 48, send.at[5])
+        for p in range(2):
+            diode = dr[16 * u + 8 * p : 16 * u + 8 * p + 8, :]
+            rest = vf[p, :, at]
+            for b in range(3):
+                y = ff[b, p, :, at]
+                rest = rest - pw[b] * y
+                out[b, p, :, at] = y + inc[b, p, :, at] - pw[b] * diode
+            out[3, p, :, at] = rest * last + inc[3, p, :, at] - pw[3] * diode
+    for i, (ref, count) in enumerate(
+        ((tx1, 504), (txv, 126), (txr, 378), (hr, 112), (ds, 48))
+    ):
+        settle(ref, count, send.at[i])
 
 
 def body(currents, incident, green, port_weights, bias_level):
@@ -409,7 +432,7 @@
             pltpu.VMEM((4, 2, 8, 512), F32),
             pltpu.VMEM((8, 64), jnp.int32),
             pltpu.SMEM((4,), F32),
-            pltpu.VMEM((8, 128), F32),
+            pltpu.VMEM((16, 128), F32),
             pltpu.VMEM((4, 4, 2, 16, 1024), F32),
             pltpu.VMEM(w1.shape, BF16),
             pltpu.VMEM(e2.shape, BF16),
@@ -418,20 +441,23 @@
             pltpu.VMEM((512, 128), F32),
             pltpu.VMEM((512, 128), F32),
             pltpu.VMEM((8, 2, 32, 128), F32),
-            pltpu.VMEM((4, 128, 128), F32),
+            pltpu.VMEM((8, 128, 128), F32),
+            pltpu.VMEM((128, 128), F32),
+            pltpu.VMEM((128, 128), F32),
             pltpu.VMEM((512, 128), F32),
             pltpu.VMEM((512, 128), F32),
-            pltpu.VMEM((64, 512), F32),
-            pltpu.VMEM((4, 64, 256), F32),
-            pltpu.VMEM((4, 2, 8, 512), F32),
+            pltpu.VMEM((4, 128, 128), F32),
+            pltpu.VMEM((2, 8, 512), F32),
+            pltpu.VMEM((2, 8, 512), F32),
+            pltpu.VMEM((3, 2, 8, 512), F32),
             pltpu.VMEM((16, 128), F32),
             pltpu.VMEM((64, 128), F32),
             pltpu.VMEM((128, 128), F32),
             pltpu.VMEM((64, 128), F32),
             pltpu.VMEM((64, 128), F32),
             pltpu.SemaphoreType.DMA((13,)),
-            pltpu.SemaphoreType.DMA((7,)),
-            pltpu.SemaphoreType.DMA((7,)),
+            pltpu.SemaphoreType.DMA((6,)),
+            pltpu.SemaphoreType.DMA((6,)),
         ],
         compiler_params=pltpu.CompilerParams(
             collective_id=0, has_side_effects=True, vmem_limit_bytes=60 * 2**20

time: 58.8 us -> 55.4 us (0.942)
  Pallas kernels: 57 us -> 53.7 us
    pallas_call x1, Pallas kernels: 57 us -> 53.7 us  [body(): pl.pallas_call(kernel, out_shape=jax.ShapeDtypeStruct((4, 2, 8, 512), F32...]
where the time goes in v3:
time: 55.4 us; the launch traced here: 55.3 us
  Pallas kernels  53.7 us (97%)
  local copies, waits for them, and re-layouts  1.57 us (3%)
    pallas_call x1, Pallas kernels, body(): pl.pallas_call(kernel, out_shape=jax.ShapeDtypeStruct((4, 2, 8, 512), F32...  53.7 us
    unnamed x1, local copies, waits for them, and re-layouts  1.57 us

profile of v3, /device:TPU:1, one launch (start us, length us, event | category | flops | bytes accessed | tf_op | source)
XLA Modules:
  0.0 55.3 jit_solution(7670578292570557517)
XLA Ops:
  0.0 53.7 %shard_map.100 = f32[4,2,8,512]{3,2,1,0:T(8,128)} custom-call(f32[4,2,8,512]{3,2,1,0:T(8,128)} %bitcast.6, f32[4,2,8,512]{3,2,1,0:T(8,128)} %bitcast.7, s32[8,64]{1,0:T(8,128)} %bias_hbm.1, f32[4]{0:T(128)} %pw_hbm.1, f32[16,128]{1,0:T(8,128)} %constant.14.clone.turn_hbm, f32[4,4,2,16,1024]{4,3,2,1,0:T(8,128)} %bitcast.5, ...), custom_call_target="tpu_custom_call" | custom-call | flops 5000000000 | bytes 13000000 | tf_op jit(solution)/shard_map/pallas_call | solution.py:425
  53.8 1.6 %copy.12 = f32[1,4,2,8,512]{4,3,2,1,0:T(8,128)} copy(f32[1,4,2,8,512]{4,3,2,1,0:T(8,128)} %bitcast.4) | data formatting | bytes 262144

commit v4 on v3

--- a/solution.py
+++ b/solution.py
@@ -422,9 +422,10 @@
     w1, e2, e3, w4, turn = (jnp.asarray(t) for t in tables())
     vmem = pl.BlockSpec(memory_space=pltpu.VMEM)
     anyw = pl.BlockSpec(memory_space=pltpu.HBM)
+    args = (currents[0], incident[0], bias_level, port_weights, turn, green[0], w1, e2, e3, w4)
     out = pl.pallas_call(
         kernel,
-        out_shape=jax.ShapeDtypeStruct((4, 2, 8, 512), F32),
+        out_shape=pltpu.VMEM((4, 2, 8, 512), F32),
         in_specs=[anyw] * 10,
         out_specs=vmem,
         scratch_shapes=[
@@ -460,10 +461,10 @@
             pltpu.SemaphoreType.DMA((6,)),
         ],
         compiler_params=pltpu.CompilerParams(
-            collective_id=0, has_side_effects=True, vmem_limit_bytes=60 * 2**20
+            collective_id=0, has_side_effects=True, vmem_limit_bytes=44 * 2**20
         ),
         cost_estimate=pl.CostEstimate(flops=5 * 10**9, bytes_accessed=13 * 10**6, transcendentals=16384),
-    )(currents[0], incident[0], bias_level, port_weights, turn, green[0], w1, e2, e3, w4)
+    )(*(pltpu.with_memory_space_constraint(a, pltpu.HBM) for a in args))
     return out[None]
 
 

time: 55.4 us -> 53.9 us (0.973)
  local copies, waits for them, and re-layouts: 1.57 us -> 0.66 us
  Pallas kernels: 53.7 us -> 53.1 us
    unnamed x1, local copies, waits for them, and re-layouts: 1.57 us -> 0.66 us
    pallas_call x1, Pallas kernels: 53.7 us -> 53.1 us  [body(): pl.pallas_call(kernel, out_shape=pltpu.VMEM((4, 2, 8, 512), F32), in_spec...]
where the time goes in v4:
time: 53.9 us; the launch traced here: 53.8 us
  Pallas kernels  53.1 us (99%)
  local copies, waits for them, and re-layouts  0.66 us (1%)
    pallas_call x1, Pallas kernels, body(): pl.pallas_call(kernel, out_shape=pltpu.VMEM((4, 2, 8, 512), F32), in_spec...  53.1 us

profile of v4, /device:TPU:1, one launch (start us, length us, event | category | flops | bytes accessed | tf_op | source)
XLA Modules:
  0.0 53.8 jit_solution(11825904563070585606)
XLA Ops:
  0.0 53.1 %shard_map.100 = f32[4,2,8,512]{3,2,1,0:T(8,128)S(1)} custom-call(f32[4,2,8,512]{3,2,1,0:T(8,128)} %bitcast.6, f32[4,2,8,512]{3,2,1,0:T(8,128)} %bitcast.7, s32[8,64]{1,0:T(8,128)} %bias_hbm.1, f32[4]{0:T(128)} %pw_hbm.1, f32[16,128]{1,0:T(8,128)} %constant.14.clone.turn_hbm, f32[4,4,2,16,1024]{4,3,2,1,0:T(8,128)} %bitcast.5, ...), custom_call_target="tpu_custom_call" | custom-call | flops 5000000000 | bytes 13000000 | tf_op jit(solution)/shard_map/pallas_call | solution.py:426
  53.1 0.7 %copy.12 = f32[1,4,2,8,512]{4,3,2,1,0:T(8,128)} copy(f32[1,4,2,8,512]{4,3,2,1,0:T(8,128)S(1)} %bitcast.4) | data formatting | bytes 262144

commit v5 on v4

--- a/solution.py
+++ b/solution.py
@@ -303,6 +303,7 @@
         return r[:64] + jnp.where(left, -s, s)
 
     settle(rx1, 504, recv.at[0])
+    later = []
     for half in range(2):
         for t in range(4):
             hi, lo = split(rx1[pl.ds(4 * half + t, 64, stride=8), :])
@@ -317,7 +318,7 @@
             for q in range(8):
                 zb[q, 0, at, :], zb[q, 1, at, :] = z[q]
 
-        def keep(i, f):
+        def keep(i, f, half=half):
             for t, (re, im) in enumerate(dft8(f, 1)):
                 if t:
                     re, im = re * tc[t] - im * ts[t], im * tc[t] + re * ts[t]
@@ -338,12 +339,14 @@
                     re, im = (u, w) if c == 0 else (re + u, im + w)
                 f.append((re, im))
             if b < 3:
-                keep(b + 1, f)
+                later.append((keep, b + 1, f))
             terms = [(pw[b] * re, pw[b] * im) for re, im in f]
             port = terms if b == 0 else [(v[0] + w[0], v[1] + w[1]) for v, w in zip(port, terms)]
         keep(0, port)
         txv[pl.ds(half, 64, stride=2), :] = rows_inverse(4 * half)
     spread(2, txv, lambda d: 2 * d, rxv, 2 * row, send.at[1], recv.at[1])
+    for keep, i, f in later:
+        keep(i, f)
     for half in range(2):
         for i in range(3):
             txr[pl.ds(3 * half + i, 64, stride=8), :] = rows_inverse(4 * half + 1 + i)
@@ -401,17 +404,22 @@
     lax.fori_loop(0, 4, hand_back, 0)
 
     last = 1.0 / jnp.full((8, 128), pw[3], F32)
+    for u in range(4):
+        at = slice(128 * u, 128 * u + 128)
+        for p in range(2):
+            rest = vf[p, :, at]
+            for b in range(3):
+                y = ff[b, p, :, at]
+                rest = rest - pw[b] * y
+                out[b, p, :, at] = y + inc[b, p, :, at]
+            out[3, p, :, at] = rest * last + inc[3, p, :, at]
     settle(dr, 48, recv.at[4])
     for u in range(4):
         at = slice(128 * u, 128 * u + 128)
         for p in range(2):
             diode = dr[16 * u + 8 * p : 16 * u + 8 * p + 8, :]
-            rest = vf[p, :, at]
-            for b in range(3):
-                y = ff[b, p, :, at]
-                rest = rest - pw[b] * y
-                out[b, p, :, at] = y + inc[b, p, :, at] - pw[b] * diode
-            out[3, p, :, at] = rest * last + inc[3, p, :, at] - pw[3] * diode
+            for b in range(4):
+                out[b, p, :, at] = out[b, p, :, at] - pw[b] * diode
     for i, (ref, count) in enumerate(
         ((tx1, 504), (txv, 126), (txr, 378), (hr, 112), (ds, 48))
     ):

time: 53.9 us -> 53.8 us (level)
  no operation moved by 1% of the time
where the time goes in v5:
time: 53.8 us; the launch traced here: 53.7 us
  Pallas kernels  53 us (99%)
  local copies, waits for them, and re-layouts  0.66 us (1%)
    pallas_call x1, Pallas kernels, body(): pl.pallas_call(kernel, out_shape=pltpu.VMEM((4, 2, 8, 512), F32), in_spec...  53 us

profile of v5, /device:TPU:1, one launch (start us, length us, event | category | flops | bytes accessed | tf_op | source)
XLA Modules:
  0.0 53.7 jit_solution(10097682534887548415)
XLA Ops:
  0.0 53.0 %shard_map.100 = f32[4,2,8,512]{3,2,1,0:T(8,128)S(1)} custom-call(f32[4,2,8,512]{3,2,1,0:T(8,128)} %bitcast.6, f32[4,2,8,512]{3,2,1,0:T(8,128)} %bitcast.7, s32[8,64]{1,0:T(8,128)} %bias_hbm.1, f32[4]{0:T(128)} %pw_hbm.1, f32[16,128]{1,0:T(8,128)} %constant.14.clone.turn_hbm, f32[4,4,2,16,1024]{4,3,2,1,0:T(8,128)} %bitcast.5, ...), custom_call_target="tpu_custom_call" | custom-call | flops 5000000000 | bytes 13000000 | tf_op jit(solution)/shard_map/pallas_call | solution.py:434
  53.0 0.7 %copy.12 = f32[1,4,2,8,512]{4,3,2,1,0:T(8,128)} copy(f32[1,4,2,8,512]{4,3,2,1,0:T(8,128)S(1)} %bitcast.4) | data formatting | bytes 262144
